TPU v7x, 512 devices: a whole 4x4x16 slice. The times are simulated.
512 devices in a mesh: seq: 64 (over z, y_lo, core), kv: 8 (over y_hi, x).
Axes of the slice: x: 4, y: 4 (y_hi: 2, y_lo: 2; y = y_hi * 2 + y_lo), z: 16, core: 2. Of those that a mesh axis runs over, the one named last changes fastest.
Arguments:
- queries: bfloat16 [8192, 8192], P('seq', 'kv'), parts along dimension 1, may hold values from -4.5 to 4.5
- keys: bfloat16 [8192, 1024], P('seq', 'kv'), parts along dimension 1, may hold values from -4.5 to 4.5
- values: bfloat16 [8192, 1024], P('seq', 'kv'), parts along dimension 1, may hold values from -6 to 6
- block_order: int32 [128], replicated, may hold values from 0 to 127, each once
Outputs:
- attention: bfloat16 [8192, 8192], P('seq', 'kv'), parts along dimension 1
- row_lse: float32 [64, 8192], P('kv', 'seq'), parts along dimension 0
- column_sums: float32 [65536], P(('kv', 'seq')), parts along dimension 0
There are 8 independent parts, one for each index of `kv`. A program takes and returns all parts, laid end to end along the dimension named above; an argument that names none is the same for every part. Nothing has to cross between parts.
Inputs may be any that keep to these rules, and one draw needn't show every extreme that they name: `block_order`: every value of 0 to 127 appears once.
All inputs are finite; a program needn't handle non-finite values.
Results may differ from a plain program's by a relative error of at most 0.0047.
Values may be sent and summed in bfloat16 or wider, within the bound.
A program may use at most 64 MiB of HBM per device.

v0:
```python
import math

import jax
import jax.numpy as jnp
from jax import lax
from jax.sharding import PartitionSpec as P

BLOCK = 64


NEG_FILL = -1e30


def key_positions(block_order, first_row, count):
    row_ids = first_row + jnp.arange(count, dtype=jnp.int32)
    block_ids = row_ids // BLOCK
    one_hot = block_ids[:, None] == jnp.arange(block_order.shape[0], dtype=jnp.int32)[None, :]
    chosen = jnp.sum(jnp.where(one_hot, block_order[None, :], 0), axis=1)
    return chosen * BLOCK + row_ids % BLOCK


def tile_scores(query_heads, key_tile, query_pos, key_pos):
    factor = 1.0 / math.sqrt(key_tile.shape[1])
    scaled = (
        jnp.einsum("qhd,kd->hqk", query_heads, key_tile, preferred_element_type=jnp.float32)
        * factor
    )
    allowed = key_pos[None, :] <= query_pos[:, None]
    return jnp.where(allowed[None, :, :], scaled, NEG_FILL)


def over_tiles(update, carried, key_arrays, first_row, block_order):
    count = key_arrays[0].shape[0]
    width = math.gcd(count, 512)
    turns = count // width

    def one_turn(turn_index, running):
        offset = turn_index * width
        tiles = tuple((lax.dynamic_slice_in_dim(member, offset, width, 0) for member in key_arrays))
        key_pos = key_positions(block_order, first_row + offset, width)
        return update(running, tiles, key_pos, first_row + offset)

    return lax.fori_loop(0, turns, one_turn, carried)


def local(queries, keys, values, block_order):
    tok_rows = queries.shape[0]
    head_dim = keys.shape[1]
    head_count = queries.shape[1] // head_dim
    query_heads = queries.reshape(tok_rows, head_count, head_dim)
    own_first = lax.axis_index("seq") * tok_rows
    query_pos = key_positions(block_order, own_first, tok_rows)
    all_rows = tok_rows * lax.axis_size("seq")

    def stats_update(running, tiles, key_pos, first_row):
        top, total = running
        scores = tile_scores(query_heads, tiles[0], query_pos, key_pos)
        new_top = jnp.maximum(top, jnp.max(scores, axis=2))
        total = total * jnp.exp(top - new_top) + jnp.sum(
            jnp.exp(scores - new_top[:, :, None]), axis=2
        )
        return (new_top, total)

    def make_mix(row_lse):

        def mix_update(running, tiles, key_pos, first_row):
            accum, columns = running
            scores = tile_scores(query_heads, tiles[0], query_pos, key_pos)
            probs = jnp.exp(scores - row_lse[:, :, None])
            columns = lax.dynamic_update_slice_in_dim(
                columns, jnp.sum(probs, axis=(0, 1)), first_row, 0
            )
            accum = accum + jnp.einsum(
                "hqk,kd->qhd",
                probs.astype(jnp.bfloat16),
                tiles[1],
                preferred_element_type=jnp.float32,
            )
            return (accum, columns)

        return mix_update

    init_stats = (
        jnp.full((head_count, tok_rows), NEG_FILL, jnp.float32),
        jnp.zeros((head_count, tok_rows), jnp.float32),
    )
    init_mix = (
        jnp.zeros((tok_rows, head_count, head_dim), jnp.float32),
        jnp.zeros((all_rows,), jnp.float32),
    )
    whole_keys, whole_values = (
        lax.all_gather(keys, "seq", axis=0, tiled=True),
        lax.all_gather(values, "seq", axis=0, tiled=True),
    )
    top, total = over_tiles(stats_update, init_stats, (whole_keys,), 0, block_order)
    row_lse = top + jnp.log(total)
    accum, columns = over_tiles(
        make_mix(row_lse), init_mix, (whole_keys, whole_values), 0, block_order
    )
    attention = accum.reshape(tok_rows, head_count * head_dim).astype(jnp.bfloat16)
    column_sums = lax.psum_scatter(columns, "seq", scatter_dimension=0, tiled=True)
    return (attention, row_lse, column_sums)


def solution(mesh):
    placed = (P("seq", "kv"), P("seq", "kv"), P("seq", "kv"), P())
    return jax.shard_map(
        local,
        mesh=mesh,
        in_specs=placed,
        out_specs=(P("seq", "kv"), P("kv", "seq"), P(("kv", "seq"))),
        check_vma=False,
    )
```

profile of v0, /device:TPU:1, one launch (start us, length us, event | category | flops | bytes accessed | tf_op | source)
XLA Modules:
  0.0 542.6 jit_solution(4366825946389751583)
XLA Ops:
  7.9 1.5 copy.19
  13.6 124.4 %all-gather.5.cloned.1.call-done = bf16[8192,128]{1,0:T(8,128)(2,1)} async-done(((bf16[128,128]{1,0:T(8,128)(2,1)}), bf16[8192,128]{1,0:T(8,128)(2,1)}) %all-gather.5.cloned.1.call-update) | async-done | bytes 2097168 | tf_op jit(solution)/shard_map/all_gather | solution.py:92
  138.0 47.2 %while.36 = (s32[]{:T(128)}, f32[8,128]{1,0:T(8,128)S(1)}, f32[8,128]{1,0:T(8,128)S(1)}, s32[128]{0:T(128)}, s32[128]{0:T(128)S(1)}, /*index=5*/bf16[8192,128]{1...) while((s32[]{:T(128)}, f32[8,128]{1,0:T(8,128)S(1)}, ...), condition=%wide.region_5.6_spmd.clone, body=%wide.region_1.5_spmd.clone.sunk | while | flops 138169856 | bytes 4850866 | solution.py:43
  185.3 73.1 %all-gather.3.cloned.1.call-done = bf16[8192,128]{0,1:T(8,128)(2,1)} async-done(((bf16[128,128]{0,1:T(8,128)(2,1)}), bf16[8192,128]{0,1:T(8,128)(2,1)}) %all-gather.3.cloned.1.call-update) | async-done | bytes 2097168 | tf_op jit(solution)/shard_map/all_gather | solution.py:93
  258.4 70.2 %while.37 = (s32[]{:T(128)}, f32[128,8,128]{0,2,1:T(8,128)S(1)}, f32[8192]{0:T(1024)S(1)}, bf16[8192,128]{0,1:T(8,128)(2,1)}, s32[128]{0:T(128)}, /*index=5*/s32...) while((s32[]{:T(128)}, f32[128,8,128]{0,2,1:T(8,128)S(1)}, ...), condition=%wide.region_9.10_spmd.clone, body=%wide.region_6.9_spmd.clone.sunk | while | flops 271595520 | bytes 3824841 | solution.py:43
  259.4 1.6 fusion.47
  261.0 1.4 fusion.48
  263.8 1.6 fusion.47
  265.4 1.4 fusion.48
  268.2 1.6 fusion.47
  269.8 1.4 fusion.48
  272.6 1.6 fusion.47
  274.2 1.4 fusion.48
  277.0 1.6 fusion.47
  278.6 1.4 fusion.48
  281.3 1.6 fusion.47
  283.0 1.4 fusion.48
  285.7 1.6 fusion.47
  290.1 1.6 fusion.47
  291.7 1.4 fusion.48
  294.5 1.6 fusion.47
  298.9 1.6 fusion.47
  300.5 1.4 fusion.48
  303.3 1.6 fusion.47
  307.7 1.6 fusion.47
  312.1 1.6 fusion.47
  313.7 1.4 fusion.48
  316.4 1.6 fusion.47
  320.8 1.6 fusion.47
  322.4 1.4 fusion.48
  325.2 1.6 fusion.47
  329.4 205.8 %all-reduce = f32[8192]{0:T(1024)S(1)} all-reduce(f32[8192]{0:T(1024)S(1)} %get-tuple-element.410), channel_id=2, replica_groups=mesh['seq'=64,'kv'=8] {'seq'}, use_global_device_ids=true, to_apply=%region_10.11.clone | all-reduce | flops 8192 | bytes 65536
  (250 shorter events, 81.2 us)
Async XLA Ops:
  7.2 130.9 %all-gather.5.cloned.1.call-start = ((), (), s32[]{:S(2)}) async-start(), calls=%async_computation.1 | async-start | bytes 2129920 | tf_op jit(solution)/shard_map/all_gather | solution.py:92
  7.9 250.5 %all-gather.3.cloned.1.call-start = ((), (), s32[]{:S(2)}) async-start(), calls=%async_computation | async-start | bytes 2129920 | tf_op jit(solution)/shard_map/all_gather | solution.py:93
  328.5 207.2 %copy-start = (f32[8,128]{1,0:T(8,128)}, f32[8,128]{1,0:T(8,128)S(1)}, u32[]{:S(2)}) copy-start(f32[8,128]{1,0:T(8,128)S(1)} %get-tuple-element.741) | copy-start | bytes 12292
Sparse Core Ops, SparseCore 0:
  10.2 127.8 all-gather.4
  140.7 117.6 all-gather.2
where the time goes:
time: 547 us; the launch traced here: 543 us
  blocking collectives  206 us (38%)
  waiting for transfers between devices  198 us (36%)
  matrix products  70.8 us (13%)
  other arithmetic  41.4 us (8%)
  between operations  14.8 us (3%)
  local copies, waits for them, and re-layouts  9.99 us (2%)
    unnamed x1, blocking collectives  206 us
    all_gather x1, waiting for transfers between devices, local(): lax.all_gather(keys, 'seq', axis=0, tiled=True)  124 us
    all_gather x1, waiting for transfers between devices, local(): lax.all_gather(values, 'seq', axis=0, tiled=True)  73.1 us
    dot_general x32, matrix products, tile_scores(): jnp.einsum('qhd,kd->hqk', query_heads, key_tile, preferred_element_type=j...  47.6 us
    reduce_sum x33, other arithmetic, key_positions(): chosen = jnp.sum(jnp.where(one_hot, block_order[None, :], 0), axis=1)  29.2 us
    dot_general x16, matrix products, mix_update(): jnp.einsum('hqk,kd->qhd', probs.astype(jnp.bfloat16), tiles[1], preferred...  23.2 us
  transfers between devices with their start and end apart: 2, of which 2 were waited for; matrix products, arithmetic and copies ran while one was open for 9% of the time, Pallas kernels for 0%

commit v1 on v0

v1 whole, which is shorter than its diff:
```python
import functools
import math

import jax
import jax.numpy as jnp
from jax import lax
from jax.experimental import pallas as pl
from jax.experimental.pallas import tpu as pltpu
from jax.sharding import PartitionSpec as P

MESH = pl.DeviceIdType.MESH
F32, BF16 = jnp.float32, jnp.bfloat16
BLOCK = 64
ROWS = 128
DIM = 128
HEADS = 8
Z = 16
TILE = 256
NEG = -1e30
LOG2E = math.log2(math.e)
SCALE = LOG2E / math.sqrt(DIM)
KEYS = Z * 2 * ROWS
CHUNKS = [(0, 256)] + [(256 + 512 * (d - 1), 512) for d in range(1, 8)] + [(3840, 256)]


def place(rho):
    rho %= Z
    return 2 * rho - 1 if 1 <= rho <= 8 else (2 * (Z - rho)) % (2 * Z)


def slot(rho, other):
    return 2 * place(rho) + other


def copies_from(rho, other):
    rho %= Z
    out = []
    if other == 0:
        if rho == 0:
            return [(3, 0, 0, ROWS), (-3, 0, 0, ROWS), (0, 1, 0, ROWS), (1, 0, 0, ROWS), (-1, 0, 0, ROWS)]
        if rho == 13:
            out = [(3, 0, 0, ROWS), (1, 0, 0, ROWS), (-1, 0, 0, ROWS)]
        if rho == 3:
            out = [(-3, 0, 0, ROWS), (-1, 0, 0, ROWS), (1, 0, 0, ROWS)]
        if rho not in (5, 7, 8, 9, 11):
            out.insert(1, (0, 1, 0, ROWS))
    if rho == 10:
        out += [(2, 0, 0, 64), (1, 0, 0, ROWS), (-1, 0, 0, ROWS)]
    if rho == 6:
        out += [(-2, 0, 64, 64), (-1, 0, 0, ROWS), (1, 0, 0, ROWS)]
    return out


def all_copies():
    number, arrivals = {}, {}
    for rho in range(Z):
        for other in (0, 1):
            for dz, dy, lo, rows in copies_from(rho, other):
                key = (rho, other, dz, dy)
                number[key] = len(number)
                target = ((rho - dz) % Z, other ^ dy)
                arrivals.setdefault(target, []).append((number[key], lo, rows))
    return number, arrivals


NUMBER, ARRIVALS = all_copies()
COPIES = len(NUMBER)
SEM_COL = 2 * COPIES
SEM_Q = SEM_COL + 32
SEM_LSE = SEM_Q + 1
SEM_OUT = SEM_LSE + 1
SEMS = SEM_OUT + 4


def dot_nt(a, b):
    return lax.dot_general(a, b, (((1,), (1,)), ((), ())), preferred_element_type=F32)


def iota(shape, axis):
    return lax.broadcasted_iota(jnp.int32, shape, axis)


def kernel(
    q_ref, k_ref, v_ref, order_ref, att_ref, lse_ref, col_ref,
    kbuf, vbuf, qd, qb, hot, ex, m_s, l_s, f_s, ot, vt, cs, csr, lpart, lrecv, obuf, orecv, send, recv,
):
    me = lax.axis_index("seq")
    z, y, c = me // 4, (me // 2) % 2, me % 2

    def device(dz, dy, dc):
        zz = lax.rem(z + dz + Z, Z)
        yy = 1 - y if dy else y
        cc = 1 - c if dc else c
        return {"seq": zz * 4 + yy * 2 + cc}

    barrier = pltpu.get_barrier_semaphore()
    partners = [(d, 0, 0) for d in (-3, -2, -1, 1, 2, 3)] + [(0, 1, 0), (0, 0, 1)]
    for p in partners:
        pl.semaphore_signal(barrier, inc=1, device_id=device(*p), device_id_type=MESH)

    def remote(src, dst, index, target):
        return pltpu.make_async_remote_copy(
            src_ref=src, dst_ref=dst, send_sem=send.at[index], recv_sem=recv.at[index],
            device_id=target, device_id_type=MESH,
        )

    bufs = (kbuf, vbuf)
    pending = []

    def block_copy(a, rho, other, dz, dy, lo, rows):
        src = slot(rho, other) * ROWS + lo
        dst = slot(rho - dz, other ^ dy) * ROWS + lo
        return remote(
            bufs[a].at[pl.ds(src, rows)], bufs[a].at[pl.ds(dst, rows)],
            a * COPIES + NUMBER[(rho % Z, other, dz, dy)], device(dz, dy, 0),
        )

    def forward(a, rho, other):
        for dz, dy, lo, rows in copies_from(rho, other):
            cp = block_copy(a, rho, other, dz, dy, lo, rows)
            cp.start()
            pending.append(cp)

    waited = set()

    def arrive(a, rho, other, then_forward=True):
        rho %= Z
        if (a, rho, other) in waited:
            return
        waited.add((a, rho, other))
        for index, lo, rows in ARRIVALS[(rho, other)]:
            here = bufs[a].at[pl.ds(slot(rho, other) * ROWS + lo, rows)]
            remote(here, here, a * COPIES + index, device(0, 1, 0)).wait_recv()
        if then_forward:
            forward(a, rho, other)

    kbuf[0:ROWS, :] = k_ref[...]
    vbuf[0:ROWS, :] = v_ref[...]
    for h in range(HEADS):
        part = q_ref[:, h * DIM:(h + 1) * DIM].astype(F32)
        qd[h // 2, :, (h % 2) * ROWS:(h % 2 + 1) * ROWS] = jnp.transpose(part).astype(BF16)

    order = order_ref[...]
    row = iota((128, 128), 0)
    lane = iota((128, 128), 1)
    at = row // 4
    rho = jnp.where(at % 2 == 1, (at + 1) // 2, Z - at // 2)
    src_z = (z + rho) % Z
    src_y = jnp.where((row // 2) % 2 == 1, 1 - y, y)
    index = 2 * (src_z * 4 + src_y * 2 + c) + row % 2
    key_block = jnp.sum(jnp.where(lane == index, order, 0), axis=1, keepdims=True)
    half = (iota((1, TILE), 1) % ROWS) // BLOCK
    lane1 = iota((1, 128), 1)
    for dc in (0, 1):
        first = 2 * (z * 4 + y * 2 + (1 - c if dc else c))
        b0 = jnp.sum(jnp.where(lane1 == first, order, 0), axis=1, keepdims=True)
        b1 = jnp.sum(jnp.where(lane1 == first + 1, order, 0), axis=1, keepdims=True)
        query_block = jnp.where(half == 0, b0, b1)
        bad = (key_block > query_block) & (iota((128, TILE), 0) < 64)
        bias = jnp.where(bad, NEG, 0.0).astype(BF16)
        for t in range(4):
            qb[4 * dc + t] = bias
    for r in range(0, KEYS, 512):
        hot[r:r + 512, :] = jnp.where(
            iota((512, 128), 1) == (iota((512, 128), 0) + r) // BLOCK, 1.0, 0.0
        ).astype(BF16)
    kr, qr = iota((ROWS, TILE), 0), iota((ROWS, TILE), 1) % ROWS
    tri = jnp.where((kr // BLOCK == qr // BLOCK) & (kr > qr), NEG, 0.0)

    def scores(ci):
        lo, n = CHUNKS[ci]

        def tile(t, masked):
            lhs = jnp.concatenate([kbuf[lo:lo + n, :], hot[lo:lo + n, :]], axis=1)
            rhs = jnp.concatenate([qd[t], qb[t]], axis=0)
            s = jnp.dot(lhs, rhs, preferred_element_type=F32)
            if masked:
                s = jnp.concatenate([s[:ROWS] + tri, s[ROWS:]], axis=0)
            top = jnp.max(s, axis=0, keepdims=True) * SCALE
            p = jnp.exp2(s * SCALE - top)
            m_s[ci, t] = top
            l_s[ci, t] = jnp.sum(p, axis=0, keepdims=True)
            ex[t, lo:lo + n, :] = p.astype(BF16)

        @pl.loop(0, 4)
        def _(t):
            tile(t, ci == 0)

        @pl.loop(4, 8)
        def _(t):
            tile(t, False)

    def column(ci):
        lo, n = CHUNKS[ci]
        pick = iota((16, TILE), 0)
        total = jnp.zeros((16, n), F32)
        for t in range(8):
            f = f_s[ci, t]
            high = f.astype(BF16).astype(F32)
            w = jnp.where(pick == 0, high, jnp.where(pick == 1, f - high, 0.0)).astype(BF16)
            total = total + dot_nt(w, ex[t, lo:lo + n, :])
        total = total[0:1] + total[1:2]
        for b in range(n // ROWS):
            cs[lo // ROWS + b] = total[:, b * ROWS:(b + 1) * ROWS]

    def send_column(rho, other):
        here, there = slot(rho, other), slot(-rho, other)
        cp = remote(cs.at[here], csr.at[there], SEM_COL + there, device(rho % Z, other, 0))
        cp.start()
        pending.append(cp)

    def mix(ci, start):
        lo, n = CHUNKS[ci]
        vt[:, 0:n] = jnp.transpose(vbuf[lo:lo + n, :].astype(F32)).astype(BF16)

        @pl.loop(0, 8)
        def _(t):
            o = jnp.dot(vt[:, 0:n], ex[t, lo:lo + n, :], preferred_element_type=F32) * f_s[ci, t]
            if start:
                ot[t] = o
            else:
                ot[t] += o

    pl.semaphore_wait(barrier, len(partners))

    forward(0, 0, 0)
    q_copy = remote(qd.at[pl.ds(0, 4)], qd.at[pl.ds(4, 4)], SEM_Q, device(0, 0, 1))
    q_copy.start()
    forward(1, 0, 0)

    def both(a, d, other):
        arrive(a, d, other)
        arrive(a, -d, other)

    q_copy.wait_recv()
    arrive(0, 0, 1)
    scores(0)
    both(0, 3, 0)
    both(0, 1, 0)
    both(0, 1, 1)
    scores(1)
    both(1, 3, 0)
    both(1, 1, 0)
    both(0, 3, 1)
    both(0, 6, 0)
    both(0, 4, 0)
    both(0, 2, 0)
    scores(3)
    both(0, 6, 1)
    both(1, 6, 0)
    both(0, 2, 1)
    scores(2)
    both(1, 4, 0)
    both(1, 2, 0)
    scores(6)
    both(0, 4, 1)
    scores(4)
    both(1, 6, 1)
    both(0, 5, 0)
    both(0, 5, 1)
    scores(5)
    both(0, 7, 0)
    both(0, 7, 1)
    scores(7)
    arrive(0, 8, 0)
    arrive(0, 8, 1)
    scores(8)

    top = m_s[0]
    for ci in range(1, 9):
        top = jnp.maximum(top, m_s[ci])
    total = l_s[0] * jnp.exp2(m_s[0] - top)
    for ci in range(1, 9):
        total = total + l_s[ci] * jnp.exp2(m_s[ci] - top)
    lpart[...] = top + jnp.log(total) * LOG2E
    l_copy = remote(lpart, lrecv, SEM_LSE, device(0, 0, 1))
    l_copy.start()
    l_copy.wait_recv()
    for t in range(8):
        a, b = lpart[t], lrecv[(t + 4) % 8]
        top = jnp.maximum(a, b)
        lse = top + jnp.log(jnp.exp2(a - top) + jnp.exp2(b - top)) * LOG2E
        for ci in range(9):
            f_s[ci, t] = jnp.exp2(m_s[ci, t] - lse)
        if t < 4:
            for h in range(2):
                lse_ref[2 * t + h:2 * t + h + 1, :] = lse[:, h * ROWS:(h + 1) * ROWS] / LOG2E

    for ci in range(8, -1, -1):
        column(ci)
        for d in ((ci,) if ci in (0, 8) else (ci, -ci)):
            for other in (0, 1):
                if (d, other) != (0, 0):
                    send_column(d, other)

    for step, ci in enumerate((0, 1, 3, 2, 4, 6, 5, 7, 8)):
        for d in ((ci,) if ci in (0, 8) else (ci, -ci)):
            for other in (0, 1):
                if (d, other) != (0, 0):
                    arrive(1, d, other)
        mix(ci, step == 0)

    out_copies = []
    for t in range(4):
        obuf[t] = ot[4 + t].astype(BF16)
        cp = remote(obuf.at[t], orecv.at[t], SEM_OUT + t, device(0, 0, 1))
        cp.start()
        out_copies.append(cp)
    for t in range(4):
        out_copies[t].wait_recv()
        o = ot[t] + orecv[t].astype(F32)
        for h in range(2):
            at = (2 * t + h) * DIM
            att_ref[:, at:at + DIM] = jnp.transpose(o[:, h * ROWS:(h + 1) * ROWS]).astype(BF16)

    total = cs[0]
    for s in range(1, 32):
        remote(cs.at[s], csr.at[s], SEM_COL + s, device(0, 1, 0)).wait_recv()
        total = total + csr[s]
    col_ref[...] = total
    for cp in pending + [q_copy, l_copy] + out_copies:
        cp.wait_send()


def local(queries, keys, values, block_order):
    vmem = pl.BlockSpec(memory_space=pltpu.VMEM)
    attention, row_lse, columns = pl.pallas_call(
        kernel,
        out_shape=(
            jax.ShapeDtypeStruct((ROWS, HEADS * DIM), BF16),
            jax.ShapeDtypeStruct((HEADS, ROWS), F32),
            jax.ShapeDtypeStruct((1, ROWS), F32),
        ),
        in_specs=[vmem] * 4,
        out_specs=(vmem,) * 3,
        scratch_shapes=[
            pltpu.VMEM((KEYS, DIM), BF16),
            pltpu.VMEM((KEYS, DIM), BF16),
            pltpu.VMEM((8, DIM, TILE), BF16),
            pltpu.VMEM((8, 128, TILE), BF16),
            pltpu.VMEM((KEYS, 128), BF16),
            pltpu.VMEM((8, KEYS, TILE), BF16),
            pltpu.VMEM((9, 8, 1, TILE), F32),
            pltpu.VMEM((9, 8, 1, TILE), F32),
            pltpu.VMEM((9, 8, 1, TILE), F32),
            pltpu.VMEM((8, DIM, TILE), F32),
            pltpu.VMEM((DIM, 512), BF16),
            pltpu.VMEM((32, 1, ROWS), F32),
            pltpu.VMEM((32, 1, ROWS), F32),
            pltpu.VMEM((8, 1, TILE), F32),
            pltpu.VMEM((8, 1, TILE), F32),
            pltpu.VMEM((4, DIM, TILE), BF16),
            pltpu.VMEM((4, DIM, TILE), BF16),
            pltpu.SemaphoreType.DMA((SEMS,)),
            pltpu.SemaphoreType.DMA((SEMS,)),
        ],
        compiler_params=pltpu.CompilerParams(
            collective_id=0, has_side_effects=True, vmem_limit_bytes=52 * 2**20
        ),
        cost_estimate=pl.CostEstimate(flops=9 * 10**9, bytes_accessed=10**6, transcendentals=9 * 10**6),
    )(queries, keys, values, block_order.reshape(1, -1))
    return attention, row_lse, columns.reshape(ROWS)


def solution(mesh):
    placed = (P("seq", "kv"), P("seq", "kv"), P("seq", "kv"), P())
    return jax.shard_map(
        local,
        mesh=mesh,
        in_specs=placed,
        out_specs=(P("seq", "kv"), P("kv", "seq"), P(("kv", "seq"))),
        check_vma=False,
    )
```

time: 547 us -> 85.6 us (0.16)
  blocking collectives: 206 us -> 0 us
  waiting for transfers between devices: 198 us -> 0 us
  Pallas kernels: 0 us -> 79.7 us
  matrix products: 70.8 us -> 0 us
  other arithmetic: 41.4 us -> 0 us
  between operations: 14.8 us -> 0.65 us
    unnamed x1 -> x0, blocking collectives: 206 us -> none
    all_gather x2 -> x0, waiting for transfers between devices: 198 us -> none  [the longest x1 124 us: local(): lax.all_gather(keys, 'seq', axis=0, tiled=True)]
    pallas_call x0 -> x1, Pallas kernels: none -> 79.7 us  [local(): pl.pallas_call(kernel, out_shape=(jax.ShapeDtypeStruct((ROWS, HEADS * DIM...]
    dot_general x48 -> x0, matrix products: 70.8 us -> none  [the longest x32 47.6 us: tile_scores(): jnp.einsum('qhd,kd->hqk', query_heads, key_tile, preferred_element_type=j...]
    reduce_sum x49 -> x0, other arithmetic: 36.3 us -> none  [the longest x33 29.2 us: key_positions(): chosen = jnp.sum(jnp.where(one_hot, block_order[None, :], 0), axis=1)]
  transfers between devices with their start and end apart: 2 -> 0, of which waited for: 2 -> 0; matrix products, arithmetic and copies ran while one was open for 9% -> 0% of each run, Pallas kernels for 0% -> 0%
where the time goes in v1:
time: 85.6 us; the launch traced here: 85.3 us
  Pallas kernels  79.7 us (93%)
  local copies, waits for them, and re-layouts  4.92 us (6%)
    pallas_call x1, Pallas kernels, local(): pl.pallas_call(kernel, out_shape=(jax.ShapeDtypeStruct((ROWS, HEADS * DIM...  79.7 us
    unnamed x11, local copies, waits for them, and re-layouts  4.92 us

profile of v1, /device:TPU:1, one launch (start us, length us, event | category | flops | bytes accessed | tf_op | source)
XLA Modules:
  0.0 85.3 jit_solution(9271920620308203896)
XLA Ops:
  0.6 0.0 copy-start.3
  0.6 0.6 copy-done.3
  1.3 0.0 copy-start
  1.3 0.9 %copy-done = bf16[128,1024]{1,0:T(8,128)(2,1)S(1)} copy-done((bf16[128,1024]{1,0:T(8,128)(2,1)S(1)}, bf16[128,1024]{1,0:T(8,128)(2,1)}, u32[]{:S(2)}) %copy-start) | copy-done | bytes 262168
  2.2 0.0 copy-start.1
  2.2 0.8 copy-done.1
  3.0 0.0 copy-start.2
  3.0 0.8 copy-done.2
  3.8 79.7 %shard_map.67 = (bf16[128,1024]{1,0:T(8,128)(2,1)S(1)}, f32[8,128]{1,0:T(8,128)S(1)}, f32[1,128]{1,0:T(1,128)S(1)}) custom-call(bf16[128,1024]{1,0:T(8,128)(2,1)S(1)} %copy-done, bf16[128,128]{1,0:T(8,128)(2,1)S(1)} %copy-done.1, bf16[128,128]{1,0:T(8,128)(2,1)S(1)} %copy-done.2, s32[1,128]{1,0:T(1,128)S(1)} %bitcast.2), custom_call_target="tpu_custom_call" | custom-call | flops 8999999488 | bytes 1000000 | tf_op jit(solution)/shard_map/pallas_call | solution.py:327
  83.5 0.7 copy.10
  84.2 0.6 copy.11
  84.8 0.5 copy.12
Async XLA Ops:
  0.6 0.7 copy-start.3
  1.3 0.9 %copy-start = (bf16[128,1024]{1,0:T(8,128)(2,1)S(1)}, bf16[128,1024]{1,0:T(8,128)(2,1)}, u32[]{:S(2)}) copy-start(bf16[128,1024]{1,0:T(8,128)(2,1)} %q_ref.1) | copy-start | bytes 786436
  2.2 0.8 copy-start.1
  3.0 0.8 copy-start.2

commit v2 on v0

v2 whole, which is shorter than its diff:
```python
import functools
import math

import jax
import jax.numpy as jnp
from jax import lax
from jax.experimental import pallas as pl
from jax.experimental.pallas import tpu as pltpu
from jax.sharding import PartitionSpec as P

MESH = pl.DeviceIdType.MESH
F32, BF16 = jnp.float32, jnp.bfloat16
BLOCK = 64
ROWS = 128
DIM = 128
HEADS = 8
Z = 16
TILE = 256
TILES = 16
NEG = -1e30
LOG2E = math.log2(math.e)
SCALE = LOG2E / math.sqrt(DIM)
KEYS = Z * ROWS
GROUPS = [(0, 1, -1), (3, -3), (2, -2, 4, -4), (6, -6), (5, -5), (7, -7, 8)]
ORDER = [rho for group in GROUPS for rho in group]
CHUNKS = []
for group in GROUPS:
    CHUNKS.append((sum(n for _, n in CHUNKS), ROWS * len(group)))
NC = len(CHUNKS)
PLACE = {rho % Z: at for at, rho in enumerate(ORDER)}


def slot(rho):
    return PLACE[rho % Z]


COPIES_FROM = {
    0: [(3, 0, ROWS), (-3, 0, ROWS), (1, 0, ROWS), (-1, 0, ROWS)],
    -3: [(3, 0, ROWS), (1, 0, ROWS), (-1, 0, ROWS)],
    3: [(-3, 0, ROWS), (-1, 0, ROWS), (1, 0, ROWS)],
    -6: [(2, 0, 64), (1, 0, ROWS), (-1, 0, ROWS)],
    6: [(-2, 64, 64), (-1, 0, ROWS), (1, 0, ROWS)],
}
NUMBER, ARRIVALS = {}, {}
for rho, copies in COPIES_FROM.items():
    for dz, lo, rows in copies:
        NUMBER[rho, dz] = len(NUMBER)
        ARRIVALS.setdefault((rho - dz) % Z, []).append((NUMBER[rho, dz], lo, rows))
COPIES = len(NUMBER)
SEM_COL = 2 * COPIES
SEM_Q = SEM_COL + Z
SEM_LSE = SEM_Q + 3
SEM_OUT = SEM_LSE + 3
SEMS = SEM_OUT + 12

EVENTS = [
    ("K", 3), ("K", 1), ("Q", 1), ("S", 0, 0), ("S", 0, 1), ("S", 1, 0), ("S", 1, 1), ("V", 3),
    ("Q", 2), ("S", 0, 2), ("S", 1, 2), ("K", 6), ("V", 1), ("Q", 3), ("S", 0, 3), ("S", 1, 3),
    ("K", 2), ("K", 4), ("S", 2, 0), ("S", 2, 1), ("V", 6), ("S", 2, 2), ("S", 2, 3),
    ("S", 3, 0), ("S", 3, 1), ("S", 3, 2), ("S", 3, 3),
    ("K", 5), ("S", 4, 0), ("S", 4, 1), ("S", 4, 2), ("S", 4, 3),
    ("K", 7), ("K", 8), ("S", 5, 0), ("S", 5, 1), ("S", 5, 2), ("S", 5, 3),
]

V_LAST = (2, 4, 5, 7, 8)
COLUMN_ORDER = (5, 3, 4, 2, 1, 0)


def dot_nt(a, b):
    return lax.dot_general(a, b, (((1,), (1,)), ((), ())), preferred_element_type=F32)


def add_log(a, b):
    top = jnp.maximum(a, b)
    return top + jnp.log(jnp.exp2(a - top) + jnp.exp2(b - top)) * LOG2E


def iota(shape, axis):
    return lax.broadcasted_iota(jnp.int32, shape, axis)


def kernel(
    q_hbm, k_hbm, v_hbm, order_hbm, att_ref, lse_ref, col_ref,
    qin, order_ref, kbuf, vbuf, qd, qb, hot, ex, m_s, l_s, f_s, ot, vt, cs, csr, lpart, lrecv, share,
    obuf, orecv, osum, load, send, recv,
):
    me = lax.axis_index("seq")
    z, y, c = me // 4, (me // 2) % 2, me % 2

    def device(dz, dy, dc):
        zz = lax.rem(z + dz + Z, Z)
        yy = 1 - y if dy else y
        cc = 1 - c if dc else c
        return {"seq": zz * 4 + yy * 2 + cc}

    barrier = pltpu.get_barrier_semaphore()
    partners = [(d, 0, 0) for d in (-3, -2, -1, 1, 2, 3)] + [(0, 0, 1), (0, 1, 0), (0, 1, 1)]
    for p in partners:
        pl.semaphore_signal(barrier, inc=1, device_id=device(*p), device_id_type=MESH)

    loads = [
        pltpu.make_async_copy(q_hbm, qin, load.at[0]),
        pltpu.make_async_copy(k_hbm, kbuf.at[pl.ds(0, ROWS)], load.at[1]),
        pltpu.make_async_copy(v_hbm, vbuf.at[pl.ds(0, ROWS)], load.at[2]),
        pltpu.make_async_copy(order_hbm, order_ref, load.at[3]),
    ]
    for cp in loads:
        cp.start()

    pending = []

    def remote(src, dst, index, target):
        return pltpu.make_async_remote_copy(
            src_ref=src, dst_ref=dst, send_sem=send.at[index], recv_sem=recv.at[index],
            device_id=target, device_id_type=MESH,
        )

    def push(*args):
        cp = remote(*args)
        cp.start()
        pending.append(cp)

    bufs = (kbuf, vbuf)

    def forward(a, rho):
        for dz, lo, rows in COPIES_FROM.get(rho, ()):
            push(
                bufs[a].at[pl.ds(slot(rho) * ROWS + lo, rows)],
                bufs[a].at[pl.ds(slot(rho - dz) * ROWS + lo, rows)],
                a * COPIES + NUMBER[rho, dz], device(dz, 0, 0),
            )

    def arrive(a, rho):
        for index, lo, rows in ARRIVALS[rho % Z]:
            here = bufs[a].at[pl.ds(slot(rho) * ROWS + lo, rows)]
            remote(here, here, a * COPIES + index, device(1, 0, 0)).wait_recv()
        forward(a, rho)

    for r in range(0, KEYS, 512):
        hot[r:r + 512, :] = jnp.where(
            iota((512, 128), 1) == (iota((512, 128), 0) + r) // BLOCK, 1.0, 0.0
        ).astype(BF16)
    row, lane, lane1 = iota((128, 128), 0), iota((128, 128), 1), iota((1, 128), 1)
    rho = jnp.zeros((128, 128), jnp.int32)
    for at, value in enumerate(ORDER):
        rho = jnp.where(row // 2 == at, value % Z, rho)
    index = 2 * (((z + rho) % Z) * 4 + y * 2 + c) + row % 2
    kr, qr = iota((ROWS, TILE), 0), iota((ROWS, TILE), 1) % ROWS
    tri = jnp.where((kr // BLOCK == qr // BLOCK) & (kr > qr), NEG, 0.0)
    half = (iota((1, TILE), 1) % ROWS) // BLOCK
    loads[3].wait()
    order = order_ref[...]
    key_block = jnp.sum(jnp.where(lane == index, order, 0), axis=1, keepdims=True)
    for g in range(4):
        yy = 1 - y if g // 2 else y
        cc = 1 - c if g % 2 else c
        first = 2 * (z * 4 + yy * 2 + cc)
        b0 = jnp.sum(jnp.where(lane1 == first, order, 0), axis=1, keepdims=True)
        b1 = jnp.sum(jnp.where(lane1 == first + 1, order, 0), axis=1, keepdims=True)
        query_block = jnp.where(half == 0, b0, b1)
        bad = (key_block > query_block) & (iota((128, TILE), 0) < 2 * Z)
        qb[g] = jnp.where(bad, NEG, 0.0).astype(BF16)
    loads[0].wait()
    for h in range(HEADS):
        part = qin[:, h * DIM:(h + 1) * DIM].astype(F32)
        qd[h // 2, :, (h % 2) * ROWS:(h % 2 + 1) * ROWS] = jnp.transpose(part).astype(BF16)
    loads[1].wait()
    loads[2].wait()

    def scores(ci, g):
        lo, n = CHUNKS[ci]
        for t in range(4 * g, 4 * g + 4):
            lhs = jnp.concatenate([kbuf[lo:lo + n, :], hot[lo:lo + n, :]], axis=1)
            rhs = jnp.concatenate([qd[t], qb[g]], axis=0)
            s = jnp.dot(lhs, rhs, preferred_element_type=F32)
            if ci == 0 and g == 0:
                s = jnp.concatenate([s[:ROWS] + tri, s[ROWS:]], axis=0)
            top = jnp.max(s, axis=0, keepdims=True) * SCALE
            p = jnp.exp2(s * SCALE - top)
            m_s[ci, t] = top
            l_s[ci, t] = jnp.sum(p, axis=0, keepdims=True)
            ex[t, lo:lo + n, :] = p.astype(BF16)

    def column(ci):
        lo, n = CHUNKS[ci]
        pick = iota((16, TILE), 0)
        total = jnp.zeros((16, n), F32)
        for t in range(TILES):
            f = f_s[ci, t]
            high = f.astype(BF16).astype(F32)
            w = jnp.where(pick == 0, high, jnp.where(pick == 1, f - high, 0.0)).astype(BF16)
            total = total + dot_nt(w, ex[t, lo:lo + n, :])
        total = total[0:1] + total[1:2]
        for b in range(n // ROWS):
            cs[lo // ROWS + b] = total[:, b * ROWS:(b + 1) * ROWS]
        for rho in GROUPS[ci]:
            if rho:
                push(cs.at[slot(rho)], csr.at[slot(-rho)], SEM_COL + slot(-rho), device(rho % Z, 0, 0))

    def mix(t):
        total = None
        for ci, (lo, n) in enumerate(CHUNKS):
            o = jnp.dot(vt[:, lo:lo + n], ex[t, lo:lo + n, :], preferred_element_type=F32)
            o = o * jnp.exp2(m_s[ci, t] - lpart[t])
            total = o if total is None else total + o
        return total

    queries = [
        remote(qd.at[pl.ds(0, 4)], qd.at[pl.ds(4, 4)], SEM_Q, device(0, 0, 1)),
        remote(qd.at[pl.ds(0, 4)], qd.at[pl.ds(8, 4)], SEM_Q + 1, device(0, 1, 0)),
        remote(qd.at[pl.ds(8, 4)], qd.at[pl.ds(12, 4)], SEM_Q + 2, device(0, 0, 1)),
    ]
    pending.extend(queries)

    pl.semaphore_wait(barrier, len(partners))

    forward(0, 0)
    queries[1].start()
    queries[0].start()
    forward(1, 0)
    for what, *at in EVENTS:
        if what == "S":
            scores(*at)
        elif what == "Q":
            queries[at[0] - 1].wait_recv()
            if at[0] == 2:
                queries[2].start()
        else:
            arrive("KV".index(what), at[0])
            if at[0] != 8:
                arrive("KV".index(what), -at[0])

    for t in range(TILES):
        top = m_s[0, t]
        for ci in range(1, NC):
            top = jnp.maximum(top, m_s[ci, t])
        total = l_s[0, t] * jnp.exp2(m_s[0, t] - top)
        for ci in range(1, NC):
            total = total + l_s[ci, t] * jnp.exp2(m_s[ci, t] - top)
        lpart[t] = top + jnp.log(total) * LOG2E
    lses = [remote(lpart, lrecv.at[g - 1], SEM_LSE + g - 1, device(0, g // 2, g % 2)) for g in (3, 2, 1)]
    for cp in lses:
        cp.start()
    pending.extend(lses)
    for rho in V_LAST:
        arrive(1, rho)
        if rho != 8:
            arrive(1, -rho)
    for ci, (lo, n) in enumerate(CHUNKS):
        vt[:, lo:lo + n] = jnp.transpose(vbuf[lo:lo + n, :].astype(F32)).astype(BF16)

    def out_copy(kind, t):
        src = (obuf.at[t], obuf.at[4 + t], osum.at[t])[kind]
        return remote(src, orecv.at[4 * kind + t], SEM_OUT + 4 * kind + t, device(0, *((0, 1), (0, 1), (1, 0))[kind]))

    outs = [[out_copy(kind, t) for t in range(4)] for kind in range(3)]
    for t in range(4):
        obuf[t] = mix(12 + t).astype(BF16)
        outs[0][t].start()
    for t in range(4):
        ot[t] = mix(8 + t)
    lses[2].wait_recv()
    for t in range(4):
        a, b = lpart[8 + t], lrecv[0, 12 + t]
        two = add_log(a, b)
        outs[0][t].wait_recv()
        osum[t] = (ot[t] * jnp.exp2(a - two) + orecv[t].astype(F32) * jnp.exp2(b - two)).astype(BF16)
        outs[2][t].start()
    for t in range(4):
        obuf[4 + t] = mix(4 + t).astype(BF16)
        outs[1][t].start()
    lses[1].wait_recv()
    lses[0].wait_recv()
    for t in range(TILES):
        g = t // 4
        parts = [lpart[t]] + [lrecv[o - 1, (o ^ g) * 4 + t % 4] for o in (1, 2, 3)]
        pair = add_log(parts[2], parts[3])
        lse = add_log(add_log(parts[0], parts[1]), pair)
        for ci in range(NC):
            f_s[ci, t] = jnp.exp2(m_s[ci, t] - lse)
        if t < 4:
            share[0, t] = jnp.exp2(parts[0] - lse)
            share[1, t] = jnp.exp2(parts[1] - lse)
            share[2, t] = jnp.exp2(pair - lse)
            for h in range(2):
                lse_ref[2 * t + h:2 * t + h + 1, :] = lse[:, h * ROWS:(h + 1) * ROWS] / LOG2E
    for ci in COLUMN_ORDER:
        column(ci)
    for t in range(4):
        ot[t] = mix(t)
    for t in range(4):
        outs[1][t].wait_recv()
        outs[2][t].wait_recv()
        o = (
            ot[t] * share[0, t] + orecv[4 + t].astype(F32) * share[1, t] + orecv[8 + t].astype(F32) * share[2, t]
        )
        for h in range(2):
            at = (2 * t + h) * DIM
            att_ref[:, at:at + DIM] = jnp.transpose(o[:, h * ROWS:(h + 1) * ROWS]).astype(BF16)

    total = cs[0]
    for s in range(1, Z):
        remote(cs.at[s], csr.at[s], SEM_COL + s, device(1, 0, 0)).wait_recv()
        total = total + csr[s]
    col_ref[...] = total
    for cp in pending + outs[0] + outs[1] + outs[2]:
        cp.wait_send()


def local(queries, keys, values, block_order):
    vmem = pl.BlockSpec(memory_space=pltpu.VMEM)
    hbm = pl.BlockSpec(memory_space=pltpu.HBM)
    attention, row_lse, columns = pl.pallas_call(
        kernel,
        out_shape=(
            jax.ShapeDtypeStruct((ROWS, HEADS * DIM), BF16),
            jax.ShapeDtypeStruct((HEADS, ROWS), F32),
            jax.ShapeDtypeStruct((1, ROWS), F32),
        ),
        in_specs=[hbm] * 4,
        out_specs=(vmem,) * 3,
        scratch_shapes=[
            pltpu.VMEM((ROWS, HEADS * DIM), BF16),
            pltpu.VMEM((1, 128), jnp.int32),
            pltpu.VMEM((KEYS, DIM), BF16),
            pltpu.VMEM((KEYS, DIM), BF16),
            pltpu.VMEM((TILES, DIM, TILE), BF16),
            pltpu.VMEM((4, 128, TILE), BF16),
            pltpu.VMEM((KEYS, 128), BF16),
            pltpu.VMEM((TILES, KEYS, TILE), BF16),
            pltpu.VMEM((NC, TILES, 1, TILE), F32),
            pltpu.VMEM((NC, TILES, 1, TILE), F32),
            pltpu.VMEM((NC, TILES, 1, TILE), F32),
            pltpu.VMEM((4, DIM, TILE), F32),
            pltpu.VMEM((DIM, KEYS), BF16),
            pltpu.VMEM((Z, 1, ROWS), F32),
            pltpu.VMEM((Z, 1, ROWS), F32),
            pltpu.VMEM((TILES, 1, TILE), F32),
            pltpu.VMEM((3, TILES, 1, TILE), F32),
            pltpu.VMEM((3, 4, 1, TILE), F32),
            pltpu.VMEM((8, DIM, TILE), BF16),
            pltpu.VMEM((12, DIM, TILE), BF16),
            pltpu.VMEM((4, DIM, TILE), BF16),
            pltpu.SemaphoreType.DMA((4,)),
            pltpu.SemaphoreType.DMA((SEMS,)),
            pltpu.SemaphoreType.DMA((SEMS,)),
        ],
        compiler_params=pltpu.CompilerParams(
            collective_id=0, has_side_effects=True, vmem_limit_bytes=63 * 2**20
        ),
        cost_estimate=pl.CostEstimate(flops=9 * 10**9, bytes_accessed=10**6, transcendentals=9 * 10**6),
    )(queries, keys, values, block_order.reshape(1, -1))
    return attention, row_lse, columns.reshape(ROWS)


def solution(mesh):
    placed = (P("seq", "kv"), P("seq", "kv"), P("seq", "kv"), P())
    return jax.shard_map(
        local,
        mesh=mesh,
        in_specs=placed,
        out_specs=(P("seq", "kv"), P("kv", "seq"), P(("kv", "seq"))),
        check_vma=False,
    )
```

time: 547 us -> 54.7 us (0.10)
  blocking collectives: 206 us -> 0 us
  waiting for transfers between devices: 198 us -> 0 us
  matrix products: 70.8 us -> 0 us
  Pallas kernels: 0 us -> 51 us
  other arithmetic: 41.4 us -> 0 us
  between operations: 14.8 us -> 0.65 us
  local copies, waits for them, and re-layouts: 9.99 us -> 2.86 us
    unnamed x1 -> x0, blocking collectives: 206 us -> none
    all_gather x2 -> x0, waiting for transfers between devices: 198 us -> none  [the longest x1 124 us: local(): lax.all_gather(keys, 'seq', axis=0, tiled=True)]
    dot_general x48 -> x0, matrix products: 70.8 us -> none  [the longest x32 47.6 us: tile_scores(): jnp.einsum('qhd,kd->hqk', query_heads, key_tile, preferred_element_type=j...]
    pallas_call x0 -> x1, Pallas kernels: none -> 51 us  [local(): pl.pallas_call(kernel, out_shape=(jax.ShapeDtypeStruct((ROWS, HEADS * DIM...]
    reduce_sum x49 -> x0, other arithmetic: 36.3 us -> none  [the longest x33 29.2 us: key_positions(): chosen = jnp.sum(jnp.where(one_hot, block_order[None, :], 0), axis=1)]
  transfers between devices with their start and end apart: 2 -> 0, of which waited for: 2 -> 0; matrix products, arithmetic and copies ran while one was open for 9% -> 0% of each run, Pallas kernels for 0% -> 0%
where the time goes in v2:
time: 54.7 us; the launch traced here: 54.5 us
  Pallas kernels  51 us (93%)
  local copies, waits for them, and re-layouts  2.86 us (5%)
  between operations  0.65 us (1%)
    pallas_call x1, Pallas kernels, local(): pl.pallas_call(kernel, out_shape=(jax.ShapeDtypeStruct((ROWS, HEADS * DIM...  51 us
    unnamed x7, local copies, waits for them, and re-layouts  2.86 us

profile of v2, /device:TPU:1, one launch (start us, length us, event | category | flops | bytes accessed | tf_op | source)
XLA Modules:
  0.0 54.5 jit_solution(14317014426722617728)
XLA Ops:
  0.6 51.0 %shard_map.67 = (bf16[128,1024]{1,0:T(8,128)(2,1)}, f32[8,128]{1,0:T(8,128)}, f32[1,128]{1,0:T(1,128)}) custom-call(bf16[128,1024]{1,0:T(8,128)(2,1)} %q_hbm.1, bf16[128,128]{1,0:T(8,128)(2,1)} %k_hbm.1, bf16[128,128]{1,0:T(8,128)(2,1)} %v_hbm.1, s32[1,128]{1,0:T(1,128)} %bitcast.2), custom_call_target="tpu_custom_call" | custom-call | flops 8999999488 | bytes 1000000 | tf_op jit(solution)/shard_map/pallas_call | solution.py:313
  51.6 0.0 copy-start
  51.6 1.7 %copy.10 = bf16[128,1024]{1,0:T(8,128)(2,1)} copy(bf16[128,1024]{1,0:T(8,128)(2,1)} %get-tuple-element.12) | data formatting | bytes 524288
  53.3 0.0 copy-done
  53.3 0.0 copy-start.1
  53.3 0.6 %copy.11 = f32[8,128]{1,0:T(8,128)} copy(f32[8,128]{1,0:T(8,128)S(1)} %copy-done) | data formatting | bytes 8192
  53.9 0.1 copy-done.1
  54.0 0.5 copy.12
Async XLA Ops:
  51.6 1.7 %copy-start = (f32[8,128]{1,0:T(8,128)S(1)}, f32[8,128]{1,0:T(8,128)}, u32[]{:S(2)}) copy-start(f32[8,128]{1,0:T(8,128)} %get-tuple-element.13) | copy-start | bytes 12292
  53.3 0.7 %copy-start.1 = (f32[1,128]{1,0:T(1,128)S(1)}, f32[1,128]{1,0:T(1,128)}, u32[]{:S(2)}) copy-start(f32[1,128]{1,0:T(1,128)} %get-tuple-element.8) | copy-start | bytes 1540

commit v3 on v2

--- a/solution.py
+++ b/solution.py
@@ -62,6 +62,7 @@
     ("K", 7), ("K", 8), ("S", 5, 0), ("S", 5, 1), ("S", 5, 2), ("S", 5, 3),
 ]
 
+DOT_TILES = 8
 V_LAST = (2, 4, 5, 7, 8)
 COLUMN_ORDER = (5, 3, 4, 2, 1, 0)
 
@@ -185,14 +186,21 @@
         lo, n = CHUNKS[ci]
         pick = iota((16, TILE), 0)
         total = jnp.zeros((16, n), F32)
-        for t in range(TILES):
+        for t in range(DOT_TILES):
             f = f_s[ci, t]
             high = f.astype(BF16).astype(F32)
             w = jnp.where(pick == 0, high, jnp.where(pick == 1, f - high, 0.0)).astype(BF16)
             total = total + dot_nt(w, ex[t, lo:lo + n, :])
         total = total[0:1] + total[1:2]
         for b in range(n // ROWS):
-            cs[lo // ROWS + b] = total[:, b * ROWS:(b + 1) * ROWS]
+            at = lo + b * ROWS
+            rest = jnp.zeros((ROWS, 128), F32)
+            for t in range(DOT_TILES, TILES):
+                f = f_s[ci, t]
+                for h in (0, 128):
+                    rest = rest + ex[t, at:at + ROWS, h:h + 128].astype(F32) * f[:, h:h + 128]
+            rest = jnp.sum(jnp.transpose(rest), axis=0, keepdims=True)
+            cs[at // ROWS] = total[:, b * ROWS:(b + 1) * ROWS] + rest
         for rho in GROUPS[ci]:
             if rho:
                 push(cs.at[slot(rho)], csr.at[slot(-rho)], SEM_COL + slot(-rho), device(rho % Z, 0, 0))
@@ -266,9 +274,6 @@
         outs[0][t].wait_recv()
         osum[t] = (ot[t] * jnp.exp2(a - two) + orecv[t].astype(F32) * jnp.exp2(b - two)).astype(BF16)
         outs[2][t].start()
-    for t in range(4):
-        obuf[4 + t] = mix(4 + t).astype(BF16)
-        outs[1][t].start()
     lses[1].wait_recv()
     lses[0].wait_recv()
     for t in range(TILES):
@@ -287,6 +292,9 @@
     for ci in COLUMN_ORDER:
         column(ci)
     for t in range(4):
+        obuf[4 + t] = mix(4 + t).astype(BF16)
+        outs[1][t].start()
+    for t in range(4):
         ot[t] = mix(t)
     for t in range(4):
         outs[1][t].wait_recv()
@@ -307,16 +315,23 @@
         cp.wait_send()
 
 
+def finish(attention, row_lse, columns, attention_out, row_lse_out, columns_out):
+    attention_out[...] = attention[...]
+    row_lse_out[...] = row_lse[...]
+    columns_out[...] = columns[...]
+
+
 def local(queries, keys, values, block_order):
     vmem = pl.BlockSpec(memory_space=pltpu.VMEM)
     hbm = pl.BlockSpec(memory_space=pltpu.HBM)
-    attention, row_lse, columns = pl.pallas_call(
+    results = (
+        jax.ShapeDtypeStruct((ROWS, HEADS * DIM), BF16),
+        jax.ShapeDtypeStruct((HEADS, ROWS), F32),
+        jax.ShapeDtypeStruct((1, ROWS), F32),
+    )
+    made = pl.pallas_call(
         kernel,
-        out_shape=(
-            jax.ShapeDtypeStruct((ROWS, HEADS * DIM), BF16),
-            jax.ShapeDtypeStruct((HEADS, ROWS), F32),
-            jax.ShapeDtypeStruct((1, ROWS), F32),
-        ),
+        out_shape=results,
         in_specs=[hbm] * 4,
         out_specs=(vmem,) * 3,
         scratch_shapes=[
@@ -350,6 +365,14 @@
         ),
         cost_estimate=pl.CostEstimate(flops=9 * 10**9, bytes_accessed=10**6, transcendentals=9 * 10**6),
     )(queries, keys, values, block_order.reshape(1, -1))
+    attention, row_lse, columns = pl.pallas_call(
+        finish,
+        out_shape=results,
+        in_specs=[vmem] * 3,
+        out_specs=(vmem,) * 3,
+        compiler_params=pltpu.CompilerParams(vmem_limit_bytes=63 * 2**20),
+        cost_estimate=pl.CostEstimate(flops=0, bytes_accessed=10**6, transcendentals=0),
+    )(*made)
     return attention, row_lse, columns.reshape(ROWS)
 
 

time: 54.7 us -> 50.7 us (0.927)
  local copies, waits for them, and re-layouts: 2.86 us -> 0 us
  Pallas kernels: 51 us -> 49.9 us
    unnamed x7 -> x0, local copies, waits for them, and re-layouts: 2.86 us -> none
    pallas_call x1 -> x2, Pallas kernels: 51 us -> 49.9 us  [the longest x1 48.2 us: local(): pl.pallas_call(kernel, out_shape=results, in_specs=[hbm] * 4, out_specs=(...]
where the time goes in v3:
time: 50.7 us; the launch traced here: 50.5 us
  Pallas kernels  49.9 us (98%)
  between operations  0.64 us (1%)
    pallas_call x1, Pallas kernels, local(): pl.pallas_call(kernel, out_shape=results, in_specs=[hbm] * 4, out_specs=(...  48.2 us
    pallas_call x1, Pallas kernels, local(): pl.pallas_call(finish, out_shape=results, in_specs=[vmem] * 3, out_specs=...  1.68 us

profile of v3, /device:TPU:1, one launch (start us, length us, event | category | flops | bytes accessed | tf_op | source)
XLA Modules:
  0.0 50.5 jit_solution(12524593854761777851)
XLA Ops:
  0.6 48.2 %shard_map.67 = (bf16[128,1024]{1,0:T(8,128)(2,1)}, f32[8,128]{1,0:T(8,128)}, f32[1,128]{1,0:T(1,128)}) custom-call(bf16[128,1024]{1,0:T(8,128)(2,1)} %q_hbm.1, bf16[128,128]{1,0:T(8,128)(2,1)} %k_hbm.1, bf16[128,128]{1,0:T(8,128)(2,1)} %v_hbm.1, s32[1,128]{1,0:T(1,128)} %bitcast.2), custom_call_target="tpu_custom_call" | custom-call | flops 8999999488 | bytes 1000000 | tf_op jit(solution)/shard_map/pallas_call | solution.py:332
  48.8 1.7 %shard_map.68 = (bf16[128,1024]{1,0:T(8,128)(2,1)}, f32[8,128]{1,0:T(8,128)}, f32[1,128]{1,0:T(1,128)}) custom-call(bf16[128,1024]{1,0:T(8,128)(2,1)} %get-tuple-element.9.attention, f32[8,128]{1,0:T(8,128)} %get-tuple-element.10.row_lse, f32[1,128]{1,0:T(1,128)} %get-tuple-element.11.columns), custom_call_target="tpu_custom_call" | custom-call | bytes 1000000 | tf_op jit(solution)/shard_map/pallas_call | solution.py:368

commit v4 on v3

--- a/solution.py
+++ b/solution.py
@@ -54,11 +54,11 @@
 SEMS = SEM_OUT + 12
 
 EVENTS = [
-    ("K", 3), ("K", 1), ("Q", 1), ("S", 0, 0), ("S", 0, 1), ("S", 1, 0), ("S", 1, 1), ("V", 3),
-    ("Q", 2), ("S", 0, 2), ("S", 1, 2), ("K", 6), ("V", 1), ("Q", 3), ("S", 0, 3), ("S", 1, 3),
-    ("K", 2), ("K", 4), ("S", 2, 0), ("S", 2, 1), ("V", 6), ("S", 2, 2), ("S", 2, 3),
+    ("K", 3), ("K", 1), ("Q", 1), ("S", 0, 0), ("S", 0, 1), ("S", 1, 0), ("S", 1, 1),
+    ("V", 3), ("Q", 2), ("S", 0, 2), ("S", 1, 2), ("K", 6), ("V", 1), ("Q", 3), ("S", 0, 3), ("S", 1, 3),
+    ("K", 2), ("K", 4), ("S", 2, 0), ("S", 2, 1), ("S", 2, 2), ("S", 2, 3),
     ("S", 3, 0), ("S", 3, 1), ("S", 3, 2), ("S", 3, 3),
-    ("K", 5), ("S", 4, 0), ("S", 4, 1), ("S", 4, 2), ("S", 4, 3),
+    ("V", 6), ("K", 5), ("S", 4, 0), ("S", 4, 1), ("S", 4, 2), ("S", 4, 3),
     ("K", 7), ("K", 8), ("S", 5, 0), ("S", 5, 1), ("S", 5, 2), ("S", 5, 3),
 ]
 
@@ -123,8 +123,10 @@
 
     bufs = (kbuf, vbuf)
 
-    def forward(a, rho):
+    def forward(a, rho, steps=(1, 2, 3)):
         for dz, lo, rows in COPIES_FROM.get(rho, ()):
+            if abs(dz) not in steps:
+                continue
             push(
                 bufs[a].at[pl.ds(slot(rho) * ROWS + lo, rows)],
                 bufs[a].at[pl.ds(slot(rho - dz) * ROWS + lo, rows)],
@@ -222,10 +224,12 @@
 
     pl.semaphore_wait(barrier, len(partners))
 
-    forward(0, 0)
+    forward(0, 0, (3,))
     queries[1].start()
     queries[0].start()
-    forward(1, 0)
+    forward(1, 0, (3,))
+    forward(0, 0, (1,))
+    forward(1, 0, (1,))
     for what, *at in EVENTS:
         if what == "S":
             scores(*at)

time: 50.7 us -> 49.8 us (0.982)
  Pallas kernels: 49.9 us -> 49 us
    pallas_call x1, Pallas kernels: 48.2 us -> 47.3 us  [local(): pl.pallas_call(kernel, out_shape=results, in_specs=[hbm] * 4, out_specs=(...]
where the time goes in v4:
time: 49.8 us; the launch traced here: 49.6 us
  Pallas kernels  49 us (98%)
  between operations  0.64 us (1%)
    pallas_call x1, Pallas kernels, local(): pl.pallas_call(kernel, out_shape=results, in_specs=[hbm] * 4, out_specs=(...  47.3 us
    pallas_call x1, Pallas kernels, local(): pl.pallas_call(finish, out_shape=results, in_specs=[vmem] * 3, out_specs=...  1.68 us

profile of v4, /device:TPU:1, one launch (start us, length us, event | category | flops | bytes accessed | tf_op | source)
XLA Modules:
  0.0 49.6 jit_solution(16776980633704711928)
XLA Ops:
  0.6 47.3 %shard_map.67 = (bf16[128,1024]{1,0:T(8,128)(2,1)}, f32[8,128]{1,0:T(8,128)}, f32[1,128]{1,0:T(1,128)}) custom-call(bf16[128,1024]{1,0:T(8,128)(2,1)} %q_hbm.1, bf16[128,128]{1,0:T(8,128)(2,1)} %k_hbm.1, bf16[128,128]{1,0:T(8,128)(2,1)} %v_hbm.1, s32[1,128]{1,0:T(1,128)} %bitcast.2), custom_call_target="tpu_custom_call" | custom-call | flops 8999999488 | bytes 1000000 | tf_op jit(solution)/shard_map/pallas_call | solution.py:336
  47.9 1.7 %shard_map.68 = (bf16[128,1024]{1,0:T(8,128)(2,1)}, f32[8,128]{1,0:T(8,128)}, f32[1,128]{1,0:T(1,128)}) custom-call(bf16[128,1024]{1,0:T(8,128)(2,1)} %get-tuple-element.9.attention, f32[8,128]{1,0:T(8,128)} %get-tuple-element.10.row_lse, f32[1,128]{1,0:T(1,128)} %get-tuple-element.11.columns), custom_call_target="tpu_custom_call" | custom-call | bytes 1000000 | tf_op jit(solution)/shard_map/pallas_call | solution.py:372
